TPU v7x, 32 devices: a whole 2x2x4 slice. The times are simulated.
32 devices in a mesh: tm: 4 (over y, x), pts: 8 (over z, core).
Axes of the slice: x: 2, y: 2, z: 4, core: 2. Of those that a mesh axis runs over, the one named last changes fastest.
Arguments:
- codes: bfloat16 [11520, 5120], P('tm', 'pts'), as said below
- scales: float32 [11520], P('tm'), may hold values from 0.005 to 0.015
- weights: float32 [5120], P('pts'), may hold values from 0.5 to 4
- freq_indices: int32 [64], replicated, may hold values from 0 to 127, as said below
Outputs:
- cross_spectral: float32 [64, 2, 89, 89], P('pts')
Inputs may be any that keep to these rules, and one draw needn't show every extreme that they name: `codes`: whole numbers. `freq_indices`: distinct bins.
All inputs are finite; a program needn't handle non-finite values.
Results may differ from a plain program's by a relative error of at most 0.0011.
Values may be sent and summed in bfloat16 or wider, within the bound.
A program may use at most 64 MiB of HBM per device.

v0:
```python
import math
import jax
import jax.numpy as jnp
from jax import lax
from jax.sharding import PartitionSpec as P

NFFT = 256


def make_tables(freq_indices):
    sample = jnp.arange(NFFT, dtype=jnp.int32)
    phases = freq_indices[:, None] * sample[None, :] % NFFT
    angles = phases.astype(jnp.float32) * (2.0 * math.pi / NFFT)
    hann_window = 0.5 - 0.5 * jnp.cos(sample.astype(jnp.float32) * (2.0 * math.pi / NFFT))
    cosine_table = (0.25 * hann_window[None, :] * jnp.cos(angles)).astype(jnp.bfloat16)
    sine_table = (-0.25 * hann_window[None, :] * jnp.sin(angles)).astype(jnp.bfloat16)
    return (cosine_table, sine_table)


def cross_matrices(stacked):
    blocks = stacked.shape[1] // 2
    products = jnp.einsum("fip,fjp->fij", stacked, stacked, preferred_element_type=jnp.float32)
    matrix_re = products[:, :blocks, :blocks] + products[:, blocks:, blocks:]
    matrix_im = products[:, :blocks, blocks:] - products[:, blocks:, :blocks]
    return jnp.stack([matrix_re, matrix_im], axis=1)


def per_device(codes, scales, weights, freq_indices):
    values = (codes.astype(jnp.float32) * scales[:, None]).astype(jnp.bfloat16)
    regrouped = lax.all_to_all(values, "tm", split_axis=1, concat_axis=0, tiled=True)
    point_count = regrouped.shape[1]
    own_weights = lax.dynamic_slice_in_dim(
        weights, lax.axis_index("tm") * point_count, point_count, 0
    )
    total_points = weights.shape[0] * lax.axis_size("pts")
    root_weight = jnp.sqrt(own_weights / total_points)
    cosine_table, sine_table = make_tables(freq_indices)
    hop_rows = regrouped.reshape(-1, NFFT // 2, point_count)
    windows = jnp.concatenate([hop_rows[:-1], hop_rows[1:]], axis=1)
    real_part = jnp.einsum("fn,bnp->fbp", cosine_table, windows, preferred_element_type=jnp.float32)
    imag_part = jnp.einsum("fn,bnp->fbp", sine_table, windows, preferred_element_type=jnp.float32)
    scaled_re = (real_part * root_weight[None, None, :]).astype(jnp.bfloat16)
    scaled_im = (imag_part * root_weight[None, None, :]).astype(jnp.bfloat16)
    stacked = jnp.concatenate([scaled_re, scaled_im], axis=1)
    partial_value = lax.psum_scatter(
        cross_matrices(stacked), "pts", scatter_dimension=0, tiled=True
    )
    return lax.psum(partial_value, "tm")


def solution(mesh):
    return jax.shard_map(
        per_device,
        mesh=mesh,
        in_specs=(P("tm", "pts"), P("tm"), P("pts"), P()),
        out_specs=P("pts", None, None, None),
        check_vma=False,
    )
```

profile of v0, /device:TPU:0, one launch (start us, length us, event | category | flops | bytes accessed | tf_op | source)
XLA Modules:
  0.0 320.9 jit_solution(16545950724297518855)
XLA Ops:
  6.5 0.0 copy-start
  6.5 6.2 %copy.9 = bf16[2880,640]{0,1:T(8,128)(2,1)} copy(bf16[2880,640]{1,0:T(8,128)(2,1)} %param.4) | data formatting | bytes 7372800 | tf_op args[0]
  12.7 0.0 copy-done
  12.7 4.6 %multiply_convert_fusion = bf16[2880,640]{0,1:T(8,128)(2,1)} fusion(bf16[2880,640]{0,1:T(8,128)(2,1)} %copy.9, f32[2880]{0:T(1024)S(1)} %copy-done), kind=kLoop, calls=%fused_computation.1 | loop fusion | flops 5529600 | bytes 7384320 | tf_op jit(solution)/shard_map/convert_element_type | solution.py:29
  17.3 5.2 %all-to-all-start = ((bf16[2880,4,160]{0,2,1:T(8,128)(2,1)}), bf16[2880,4,160]{0,2,1:T(8,128)(2,1)}, u32[]{:S(2)}, u32[]{:S(2)}) async-start(bf16[2880,4,160]{0,2,1:T(8,128)(2,1)} %bitcast.15), calls=%async_computation | async-start | bytes 7536640 | tf_op jit(solution)/shard_map/all_to_all | solution.py:30
  22.5 0.0 all-reduce.6.cloned.1.call-start
  22.6 0.8 multiply_sqrt_fusion
  23.3 43.1 %all-to-all-done = bf16[2880,4,160]{0,2,1:T(8,128)(2,1)} async-done(((bf16[2880,4,160]{0,2,1:T(8,128)(2,1)}), bf16[2880,4,160]{0,2,1:T(8,128)(2,1)}, u32[]{:S(2)}, u32[]{:S(2)}) %all-to-all-start) | async-done | bytes 3686432 | tf_op jit(solution)/shard_map/all_to_all | solution.py:30
  66.4 5.9 %copy.10 = bf16[4,2880,160]{1,0,2:T(4,128)(2,1)} copy(bf16[4,2880,160]{1,2,0:T(8,128)(2,1)} %bitcast.2) | data formatting | bytes 7372800 | tf_op jit(solution)/shard_map/all_to_all | solution.py:30
  72.3 8.5 %reshape.24 = bf16[90,128,160]{1,0,2:T(8,128)(2,1)} reshape(bf16[4,2880,160]{1,0,2:T(4,128)(2,1)} %copy.10) | data formatting | bytes 7372800 | tf_op jit(solution)/shard_map/reshape | solution.py:38
  80.8 0.0 copy-start.1
  80.8 4.9 %fusion.32 = (bf16[89,128,160]{1,0,2:T(8,128)(2,1)S(1)}, bf16[89,128,160]{1,0,2:T(8,128)(2,1)S(1)}) fusion(bf16[90,128,160]{1,0,2:T(8,128)(2,1)} %reshape.24), kind=kLoop, calls=%fused_computation.44 | loop fusion | bytes 14581760 | tf_op jit(solution)/shard_map/slice | solution.py:39
  85.8 0.0 copy-done.1
  85.8 3.7 %multiply_convert_fusion.2 = bf16[64,89,160]{1,0,2:T(8,128)(2,1)S(1)} fusion(f32[160]{0:T(256)S(1)} %multiply_sqrt_fusion, bf16[89,128,160]{1,0,2:T(8,128)(2,1)S(1)} %get-tuple-element.8, bf16[89,128,160]{1,0,2:T(8,128)(2,1)S(1)} %get-tuple-element.7, s32[64]{0:T(128)S(1)} %copy-done.1, f32[256]{0:T(256)S(1)} %fusion.21), kind=kOutput, calls=%fused_computation.7 | convolution fusion | flops 483282944 | bytes 9115520 | tf_op jit(solution)/shard_map/fn,bnp->fbp/dot_general | solution.py:40
  89.4 3.6 %multiply_convert_fusion.1 = bf16[64,89,160]{1,0,2:T(8,128)(2,1)S(1)} fusion(f32[160]{0:T(256)S(1)} %multiply_sqrt_fusion, bf16[89,128,160]{1,0,2:T(8,128)(2,1)S(1)} %get-tuple-element.8, bf16[89,128,160]{1,0,2:T(8,128)(2,1)S(1)} %get-tuple-element.7, f32[256]{0:T(256)S(1)} %fusion.20, s32[64]{0:T(128)S(1)} %copy-done.1), kind=kOutput, calls=%fused_computation.6 | convolution fusion | flops 483282944 | bytes 9115520 | tf_op jit(solution)/shard_map/fn,bnp->fbp/dot_general | solution.py:41
  93.1 2.2 pad_maximum_fusion.2
  95.3 17.2 %fusion = f32[64,178,178]{2,1,0:T(8,128)} fusion(bf16[64,178,160]{1,0,2:T(8,128)(2,1)S(1)} %pad_maximum_fusion.2), kind=kOutput, calls=%fused_computation.4 | convolution fusion | flops 648888320 | bytes 11756544 | tf_op jit(solution)/shard_map/fip,fjp->fij/dot_general | solution.py:22
  112.5 9.8 %fusion.5 = (f32[64,1,89,89]{3,2,0,1:T(8,128)S(1)}, f32[64,1,89,89]{3,2,0,1:T(8,128)}) fusion(f32[64,178,178]{2,1,0:T(8,128)} %fusion), kind=kLoop, calls=%fused_computation.13 | loop fusion | flops 1013888 | bytes 12166656 | tf_op jit(solution)/shard_map/stack | solution.py:25
  122.3 2.6 pad_maximum_fusion.1
  124.9 7.8 %copy.13 = f32[64,2,89,89]{3,1,2,0:T(2,128)} copy(f32[64,2,89,89]{3,2,0,1:T(8,128)S(1)} %pad_maximum_fusion.1) | data formatting | bytes 8111104 | tf_op jit(solution)/shard_map/stack | solution.py:25
  132.7 0.0 copy-start.2
  132.7 0.0 all-reduce.6.cloned.1.call-update
  132.7 0.0 all-reduce.4.cloned.1.call-start
  132.8 0.6 copy-done.2
  133.4 0.6 dynamic-slice
  134.6 126.2 %all-reduce.6.cloned.1.call-done = f32[64,2,89,89]{3,1,2,0:T(2,128)} async-done(((f32[64,2,89,89]{3,1,2,0:T(2,128)}), f32[64,2,89,89]{3,1,2,0:T(2,128)}) %all-reduce.6.cloned.1.call-update) | async-done | bytes 4055568
  260.8 2.0 constant_dynamic-slice_fusion
  262.8 0.0 all-reduce.4.cloned.1.call-update
  262.8 49.2 %all-reduce.4.cloned.1.call-done = f32[8,2,89,89]{3,1,2,0:T(2,128)} async-done(((f32[8,2,89,89]{3,1,2,0:T(2,128)}), f32[8,2,89,89]{3,1,2,0:T(2,128)}) %all-reduce.4.cloned.1.call-update) | async-done | bytes 506960 | tf_op jit(solution)/shard_map/psum | solution.py:48
  312.0 2.0 copy.18
  (2 shorter events, 0.1 us)
Async XLA Ops:
  6.5 6.2 %copy-start = (f32[2880]{0:T(1024)S(1)}, f32[2880]{0:T(1024)}, u32[]{:S(2)}) copy-start(f32[2880]{0:T(1024)} %param.5) | copy-start | bytes 34564
  17.3 49.1 %all-to-all-start = ((bf16[2880,4,160]{0,2,1:T(8,128)(2,1)}), bf16[2880,4,160]{0,2,1:T(8,128)(2,1)}, u32[]{:S(2)}, u32[]{:S(2)}) async-start(bf16[2880,4,160]{0,2,1:T(8,128)(2,1)} %bitcast.15), calls=%async_computation | async-start | bytes 7536640 | tf_op jit(solution)/shard_map/all_to_all | solution.py:30
  22.5 238.3 %all-reduce.6.cloned.1.call-start = ((), (), s32[]{:S(2)}) async-start(), calls=%async_computation.2 | async-start | bytes 11665408
  80.8 4.9 %copy-start.1 = (s32[64]{0:T(128)S(1)}, s32[64]{0:T(128)}, u32[]{:S(2)}) copy-start(s32[64]{0:T(128)} %param.7) | copy-start | bytes 772
  132.7 0.7 copy-start.2
  132.7 179.3 %all-reduce.4.cloned.1.call-start = ((), (), s32[]{:S(2)}) async-start(), calls=%async_computation.1 | async-start | bytes 1458176 | tf_op jit(solution)/shard_map/psum | solution.py:48
Sparse Core Ops, SparseCore 0:
  132.9 127.8 all-reduce.5
  263.9 48.1 all-reduce.3
where the time goes:
time: 322 us; the launch traced here: 321 us
  waiting for transfers between devices  219 us (68%)
  local copies, waits for them, and re-layouts  38.5 us (12%)
  matrix products  24.5 us (8%)
  other arithmetic  20.1 us (6%)
  between operations  14.1 us (4%)
  starting transfers between devices  5.21 us (2%)
    unnamed x3, waiting for transfers between devices  126 us
    psum x1, waiting for transfers between devices, per_device(): return lax.psum(partial_value, 'tm')  49.2 us
    all_to_all x1, waiting for transfers between devices, per_device(): lax.all_to_all(values, 'tm', split_axis=1, concat_axis=0, tiled=True)  43.1 us
    dot_general x1, matrix products, cross_matrices(): jnp.einsum('fip,fjp->fij', stacked, stacked, preferred_element_type=jnp.f...  17.2 us
    another operation x2, other arithmetic, cross_matrices(): return jnp.stack([matrix_re, matrix_im], axis=1)  12.4 us
    unnamed x10, local copies, waits for them, and re-layouts  11.4 us
    reshape x1, local copies, waits for them, and re-layouts, per_device(): hop_rows = regrouped.reshape(-1, NFFT // 2, point_count)  8.52 us
    another operation x1, local copies, waits for them, and re-layouts, cross_matrices(): return jnp.stack([matrix_re, matrix_im], axis=1)  7.81 us
  transfers between devices with their start and end apart: 3, of which 3 were waited for; matrix products, arithmetic and copies ran while one was open for 0% of the time, Pallas kernels for 0%

commit v1 on v0

--- a/solution.py
+++ b/solution.py
@@ -5,6 +5,22 @@
 from jax.sharding import PartitionSpec as P
 
 NFFT = 256
+
+
+def exchange_in_pairs(shard, axis, split, join):
+    ways, here = (lax.axis_size(axis), lax.axis_index(axis))
+    width = shard.shape[split] // ways
+    shape = list(shard.shape)
+    shape[split] = width
+    height = shape[join]
+    shape[join] = height * ways
+    full = jnp.zeros(shape, shard.dtype)
+    for mask in range(ways):
+        part = lax.dynamic_slice_in_dim(shard, (here ^ mask) * width, width, axis=split)
+        if mask:
+            part = lax.ppermute(part, axis, [(d, d ^ mask) for d in range(ways)])
+        full = lax.dynamic_update_slice_in_dim(full, part, (here ^ mask) * height, axis=join)
+    return full
 
 
 def make_tables(freq_indices):
@@ -27,7 +43,7 @@
 
 def per_device(codes, scales, weights, freq_indices):
     values = (codes.astype(jnp.float32) * scales[:, None]).astype(jnp.bfloat16)
-    regrouped = lax.all_to_all(values, "tm", split_axis=1, concat_axis=0, tiled=True)
+    regrouped = exchange_in_pairs(values, "tm", 1, 0)
     point_count = regrouped.shape[1]
     own_weights = lax.dynamic_slice_in_dim(
         weights, lax.axis_index("tm") * point_count, point_count, 0

time: 322 us -> 350 us (1.087)
  local copies, waits for them, and re-layouts: 38.5 us -> 89.8 us
  waiting for transfers between devices: 219 us -> 195 us
    all_to_all x1 -> x0, waiting for transfers between devices: 43.1 us -> none  [per_device(): lax.all_to_all(values, 'tm', split_axis=1, concat_axis=0, tiled=True)]
    dynamic_update_slice x0 -> x4, local copies, waits for them, and re-layouts: none -> 37.3 us  [exchange_in_pairs(): lax.dynamic_update_slice_in_dim(full, part, (here ^ mask) * height, axis=...]
    ppermute x0 -> x3, waiting for transfers between devices: none -> 19.1 us  [exchange_in_pairs(): part = lax.ppermute(part, axis, [(d, d ^ mask) for d in range(ways)])]
    slice x1 -> x3, local copies, waits for them, and re-layouts: 4.92 us -> 20.2 us  [per_device(): windows = jnp.concatenate([hop_rows[:-1], hop_rows[1:]], axis=1)]
    reshape x1 -> x0, local copies, waits for them, and re-layouts: 8.52 us -> none  [per_device(): hop_rows = regrouped.reshape(-1, NFFT // 2, point_count)]
    all_to_all x1 -> x0, local copies, waits for them, and re-layouts: 5.86 us -> none  [per_device(): lax.all_to_all(values, 'tm', split_axis=1, concat_axis=0, tiled=True)]
    all_to_all x1 -> x0, starting transfers between devices: 5.16 us -> none  [per_device(): lax.all_to_all(values, 'tm', split_axis=1, concat_axis=0, tiled=True)]
    unnamed x10 -> x13, local copies, waits for them, and re-layouts: 11.4 us -> 16.2 us
  transfers between devices with their start and end apart: 3 -> 5, of which waited for: 3 -> 4; matrix products, arithmetic and copies ran while one was open for 0% -> 9% of each run, Pallas kernels for 0% -> 0%
where the time goes in v1:
time: 350 us; the launch traced here: 349 us
  waiting for transfers between devices  195 us (56%)
  local copies, waits for them, and re-layouts  89.8 us (26%)
  matrix products  26.9 us (8%)
  other arithmetic  18.2 us (5%)
  between operations  14.1 us (4%)
  starting transfers between devices  4.5 us (1%)
    unnamed x3, waiting for transfers between devices  127 us
    psum x1, waiting for transfers between devices, per_device(): return lax.psum(partial_value, 'tm')  49.2 us
    dynamic_update_slice x4, local copies, waits for them, and re-layouts, exchange_in_pairs(): lax.dynamic_update_slice_in_dim(full, part, (here ^ mask) * height, axis=...  37.3 us
    slice x3, local copies, waits for them, and re-layouts, per_device(): windows = jnp.concatenate([hop_rows[:-1], hop_rows[1:]], axis=1)  20.2 us
    ppermute x3, waiting for transfers between devices, exchange_in_pairs(): part = lax.ppermute(part, axis, [(d, d ^ mask) for d in range(ways)])  19.1 us
    dot_general x1, matrix products, cross_matrices(): jnp.einsum('fip,fjp->fij', stacked, stacked, preferred_element_type=jnp.f...  17.1 us
    unnamed x13, local copies, waits for them, and re-layouts  16.2 us
    another operation x2, other arithmetic, cross_matrices(): return jnp.stack([matrix_re, matrix_im], axis=1)  12.4 us
  transfers between devices with their start and end apart: 5, of which 4 were waited for; matrix products, arithmetic and copies ran while one was open for 9% of the time, Pallas kernels for 0%

profile of v1, /device:TPU:0, one launch (start us, length us, event | category | flops | bytes accessed | tf_op | source)
XLA Modules:
  0.0 348.6 jit_solution(1986767015137077375)
XLA Ops:
  6.5 6.2 %copy.8 = bf16[2880,640]{0,1:T(8,128)(2,1)} copy(bf16[2880,640]{1,0:T(8,128)(2,1)} %param.4) | data formatting | bytes 7372800 | tf_op args[0]
  12.7 2.7 multiply_convert_fusion
  15.4 1.6 constant_dynamic-slice_fusion
  17.1 2.9 collective-permute-start
  20.0 1.5 collective-permute-start.1
  21.5 2.0 broadcast_in_dim.2
  23.6 8.9 %dynamic_update_slice.12 = bf16[11520,160]{0,1:T(8,128)(2,1)} dynamic-update-slice(bf16[11520,160]{0,1:T(8,128)(2,1)} %broadcast_in_dim.2, bf16[2880,160]{0,1:T(8,128)(2,1)S(1)} %get-tuple-element.10, s32[]{:T(128)S(6)} %select_n.34, s32[]{:T(128)} %constant.20.clone.1) | dynamic-update-slice | bytes 1843204 | tf_op jit(solution)/shard_map/dynamic_update_slice | solution.py:22
  32.6 0.8 multiply_sqrt_fusion
  33.4 8.6 %collective-permute-done = bf16[2880,160]{0,1:T(8,128)(2,1)} collective-permute-done((bf16[2880,160]{0,1:T(8,128)(2,1)}, bf16[2880,160]{0,1:T(8,128)(2,1)}, u32[]{:S(2)}, u32[]{:S(2)}) %collective-permute-start) | collective-permute-done | bytes 921632 | tf_op jit(solution)/shard_map/ppermute | solution.py:21
  42.0 10.3 %dynamic_update_slice.13 = bf16[11520,160]{0,1:T(8,128)(2,1)} dynamic-update-slice(bf16[11520,160]{0,1:T(8,128)(2,1)} %dynamic_update_slice.12, bf16[2880,160]{0,1:T(8,128)(2,1)} %collective-permute-done, s32[]{:T(128)S(6)} %select_n.36, s32[]{:T(128)} %constant.20.clone.1) | dynamic-update-slice | bytes 1843204 | tf_op jit(solution)/shard_map/dynamic_update_slice | solution.py:22
  52.3 10.5 %collective-permute-done.1 = bf16[2880,160]{0,1:T(8,128)(2,1)S(1)} collective-permute-done((bf16[2880,160]{0,1:T(8,128)(2,1)}, bf16[2880,160]{0,1:T(8,128)(2,1)S(1)}, u32[]{:S(2)}, u32[]{:S(2)}) %collective-permute-start.1) | collective-permute-done | bytes 921632 | tf_op jit(solution)/shard_map/ppermute | solution.py:21
  62.7 8.9 %dynamic_update_slice.14 = bf16[11520,160]{0,1:T(8,128)(2,1)} dynamic-update-slice(bf16[11520,160]{0,1:T(8,128)(2,1)} %dynamic_update_slice.13, bf16[2880,160]{0,1:T(8,128)(2,1)S(1)} %collective-permute-done.1, s32[]{:T(128)S(6)} %select_n.38, s32[]{:T(128)} %constant.20.clone.1) | dynamic-update-slice | bytes 1843204 | tf_op jit(solution)/shard_map/dynamic_update_slice | solution.py:22
  71.6 9.2 %dynamic_update_slice.15 = bf16[11520,160]{0,1:T(8,128)(2,1)} dynamic-update-slice(bf16[11520,160]{0,1:T(8,128)(2,1)} %dynamic_update_slice.14, bf16[2880,160]{0,1:T(8,128)(2,1)S(1)} %collective-permute-done.2, s32[]{:T(128)S(6)} %select_n.40, s32[]{:T(128)} %constant.20.clone.1) | dynamic-update-slice | bytes 1843204 | tf_op jit(solution)/shard_map/dynamic_update_slice | solution.py:22
  80.8 6.5 %fusion.28 = (bf16[11392,160]{0,1:T(8,128)(2,1)}, bf16[11392,160]{0,1:T(8,128)(2,1)}) fusion(bf16[11520,160]{0,1:T(8,128)(2,1)} %dynamic_update_slice.15), kind=kLoop, calls=%fused_computation.45 | loop fusion | bytes 14581760 | tf_op jit(solution)/shard_map/slice | solution.py:55
  87.3 6.8 %slice.25 = bf16[89,128,160]{1,0,2:T(8,128)(2,1)} reshape(bf16[11392,160]{0,1:T(8,128)(2,1)} %get-tuple-element.12) | data formatting | bytes 7290880 | tf_op jit(solution)/shard_map/slice | solution.py:55
  94.2 4.8 %constant_dynamic-update-slice_fusion.1 = bf16[89,256,160]{1,0,2:T(8,128)(2,1)} fusion(bf16[89,128,160]{1,0,2:T(8,128)(2,1)} %slice.25), kind=kLoop, calls=%fused_computation.27 | loop fusion | bytes 7577600
  99.0 6.8 %slice.27 = bf16[89,128,160]{1,0,2:T(8,128)(2,1)} reshape(bf16[11392,160]{0,1:T(8,128)(2,1)} %get-tuple-element.11) | data formatting | bytes 7290880 | tf_op jit(solution)/shard_map/slice | solution.py:55
  105.8 4.7 %constant_dynamic-update-slice_fusion = bf16[89,256,160]{1,0,2:T(8,128)(2,1)} fusion(bf16[89,256,160]{1,0,2:T(8,128)(2,1)} %constant_dynamic-update-slice_fusion.1, bf16[89,128,160]{1,0,2:T(8,128)(2,1)} %slice.27), kind=kLoop, calls=%fused_computation.26 | loop fusion | bytes 7864320 | tf_op jit(solution)/shard_map/concatenate | solution.py:55
  110.5 6.5 %multiply_convert_fusion.2 = bf16[64,89,160]{1,0,2:T(8,128)(2,1)S(1)} fusion(f32[160]{0:T(256)S(1)} %multiply_sqrt_fusion, bf16[89,256,160]{1,0,2:T(8,128)(2,1)} %constant_dynamic-update-slice_fusion, s32[64]{0:T(128)S(1)} %copy-done.2, f32[256]{0:T(256)S(1)} %fusion.21), kind=kOutput, calls=%fused_computation.6 | convolution fusion | flops 468701184 | bytes 9115520 | tf_op jit(solution)/shard_map/fn,bnp->fbp/dot_general | solution.py:56
  117.1 3.2 multiply_convert_fusion.1
  120.3 2.2 pad_maximum_fusion.1
  122.5 17.1 %fusion = f32[64,178,178]{2,1,0:T(8,128)} fusion(bf16[64,178,160]{1,0,2:T(8,128)(2,1)S(1)} %pad_maximum_fusion.1), kind=kOutput, calls=%fused_computation.3 | convolution fusion | flops 648888320 | bytes 11756544 | tf_op jit(solution)/shard_map/fip,fjp->fij/dot_general | solution.py:38
  139.6 9.8 %fusion.3 = (f32[64,1,89,89]{3,2,0,1:T(8,128)S(1)}, f32[64,1,89,89]{3,2,0,1:T(8,128)}) fusion(f32[64,178,178]{2,1,0:T(8,128)} %fusion), kind=kLoop, calls=%fused_computation.10 | loop fusion | flops 1013888 | bytes 12166656 | tf_op jit(solution)/shard_map/stack | solution.py:41
  149.5 2.6 pad_maximum_fusion
  152.1 7.8 %copy.11 = f32[64,2,89,89]{3,1,2,0:T(2,128)} copy(f32[64,2,89,89]{3,2,0,1:T(8,128)S(1)} %pad_maximum_fusion) | data formatting | bytes 8111104 | tf_op jit(solution)/shard_map/stack | solution.py:41
  159.9 0.0 all-reduce.4.cloned.1.call-start
  160.0 0.6 copy-done.3
  160.6 0.6 dynamic-slice
  161.8 126.7 %all-reduce.6.cloned.1.call-done = f32[64,2,89,89]{3,1,2,0:T(2,128)} async-done(((f32[64,2,89,89]{3,1,2,0:T(2,128)}), f32[64,2,89,89]{3,1,2,0:T(2,128)}) %all-reduce.6.cloned.1.call-update) | async-done | bytes 4055568
  288.5 2.0 constant_dynamic-slice_fusion.4
  290.6 49.2 %all-reduce.4.cloned.1.call-done = f32[8,2,89,89]{3,1,2,0:T(2,128)} async-done(((f32[8,2,89,89]{3,1,2,0:T(2,128)}), f32[8,2,89,89]{3,1,2,0:T(2,128)}) %all-reduce.4.cloned.1.call-update) | async-done | bytes 506960 | tf_op jit(solution)/shard_map/psum | solution.py:64
  339.8 2.0 copy.21
  (14 shorter events, 0.1 us)
Async XLA Ops:
  6.5 6.2 %copy-start.1 = (f32[2880]{0:T(1024)S(1)}, f32[2880]{0:T(1024)}, u32[]{:S(2)}) copy-start(f32[2880]{0:T(1024)} %param.5) | copy-start | bytes 34564
  6.5 282.0 %all-reduce.6.cloned.1.call-start = ((), (), s32[]{:S(2)}) async-start(), calls=%async_computation.1 | async-start | bytes 11665408
  17.1 25.0 %collective-permute-start = (bf16[2880,160]{0,1:T(8,128)(2,1)}, bf16[2880,160]{0,1:T(8,128)(2,1)}, u32[]{:S(2)}, u32[]{:S(2)}) collective-permute-start(bf16[2880,160]{0,1:T(8,128)(2,1)} %get-tuple-element.9), channel_id=1, source_target_pairs={{0,8},{8,0},{16,24},{24,16},{1,9},{9,1},{17,25},{25,17},{2,10},{10... | collective-permute-start | bytes 2764808 | tf_op jit(solution)/shard_map/ppermute | solution.py:21
  20.0 42.7 %collective-permute-start.1 = (bf16[2880,160]{0,1:T(8,128)(2,1)}, bf16[2880,160]{0,1:T(8,128)(2,1)S(1)}, u32[]{:S(2)}, u32[]{:S(2)}) collective-permute-start(bf16[2880,160]{0,1:T(8,128)(2,1)} %get-tuple-element.8), channel_id=1, source_target_pairs={{0,16},{8,24},{16,0},{24,8},{1,17},{9,25},{17,1},{25,9},{2,18},{10... | collective-permute-start | bytes 2764808 | tf_op jit(solution)/shard_map/ppermute | solution.py:21
  21.5 50.1 %collective-permute-start.2 = (bf16[2880,160]{0,1:T(8,128)(2,1)}, bf16[2880,160]{0,1:T(8,128)(2,1)S(1)}, u32[]{:S(2)}, u32[]{:S(2)}) collective-permute-start(bf16[2880,160]{0,1:T(8,128)(2,1)} %get-tuple-element.7), channel_id=1, source_target_pairs={{0,24},{8,16},{16,8},{24,0},{1,25},{9,17},{17,9},{25,1},{2,26},{10... | collective-permute-start | bytes 2764808 | tf_op jit(solution)/shard_map/ppermute | solution.py:21
  105.8 4.7 %copy-start.2 = (s32[64]{0:T(128)S(1)}, s32[64]{0:T(128)}, u32[]{:S(2)}) copy-start(s32[64]{0:T(128)} %param.7) | copy-start | bytes 772
  110.5 6.6 %copy-start = (bf16[89,256,160]{1,0,2:T(8,128)(2,1)S(1)}, bf16[89,256,160]{1,0,2:T(8,128)(2,1)}, u32[]{:S(2)}) copy-start(bf16[89,256,160]{1,0,2:T(8,128)(2,1)} %constant_dynamic-update-slice_fusion) | copy-start | bytes 21872644
  159.9 0.7 copy-start.3
  159.9 179.8 %all-reduce.4.cloned.1.call-start = ((), (), s32[]{:S(2)}) async-start(), calls=%async_computation | async-start | bytes 1458176 | tf_op jit(solution)/shard_map/psum | solution.py:64
Sparse Core Ops, SparseCore 0:
  160.0 128.4 all-reduce.5
  291.6 48.1 all-reduce.3
